TPU v7x, 32 devices: a whole 2x2x4 slice. The times are simulated.
32 devices in a mesh: seq: 8 (over y, x, core), tensor: 4 (over z).
Axes of the slice: x: 2, y: 2, z: 4, core: 2. Of those that a mesh axis runs over, the one named last changes fastest.
Arguments:
- tokens: bfloat16 [2048, 1024], P('seq'), may hold values from -12 to 12
- cache_keys: bfloat16 [2048, 1024], P('seq', 'tensor'), may hold values from -700 to 700
- cache_values: bfloat16 [2048, 1024], P('seq', 'tensor'), may hold values from -6 to 6
- joined_weight: float32 [1024, 3072], P(('seq', 'tensor')), may hold values from -0.1875 to 0.1875
- output_weight: float32 [1024, 1024], P(('seq', 'tensor')), may hold values from -0.1875 to 0.1875
- upward_weight: float32 [1024, 4096], P(('seq', 'tensor')), may hold values from -0.1875 to 0.1875
- downward_weight: float32 [1024, 4096], P(('seq', 'tensor')), may hold values from -0.09375 to 0.09375
- first_gain: float32 [1024], replicated, may hold values from 0.1 to 1.9
- second_gain: float32 [1024], replicated, may hold values from 0.1 to 1.9
- bias_table: float32 [32, 16], P(None, 'tensor'), may hold values from -4 to 4
- bucket_index: int32 [1023], replicated, may hold values from 0 to 31, as said below
- cached_lengths: int32 [8], replicated, may hold values from 0 to 256, as said below
- new_counts: int32 [8], replicated, may hold values from 1 to 256, as said below
- extend_flags: int32 [8], replicated, may hold values 0 or 1
Outputs:
- layer_out: bfloat16 [2048, 1024], P(('seq', 'tensor'))
Inputs may be any that keep to these rules, and one draw needn't show every extreme that they name: `cached_lengths`: some request has exactly 256 cached tokens. `new_counts`: slots of a request past its count are padding; some request fills all 256. `bucket_index`: entry 511 + o is the bucket of offset o; offsets o <= 0 take buckets below 16, offsets o > 0 the others, and on each side the bucket never falls as the distance grows.
All inputs are finite; a program needn't handle non-finite values.
Results may differ from a plain program's by a relative error of at most 0.015.
Values may be sent and summed in bfloat16 or wider, within the bound.
No kernel may reach another device: no remote copies, remote signals or barrier semaphores. Data moves between devices by JAX's collectives and lax.ppermute only.
A program may use at most 128 MiB of HBM per device.

v0:
```python
import jax
import jax.numpy as jnp
from jax import lax
from jax.sharding import PartitionSpec as P

EPSILON = 1e-06
FLOOR_SCORE = -1e30


def rms_rows(rows, gain):
    rows = rows.astype(jnp.float32)
    mean_square = jnp.mean(rows * rows, axis=-1, keepdims=True)
    return (rows * lax.rsqrt(mean_square + EPSILON) * gain).astype(jnp.bfloat16)


def row_adder(left_rows, block_rows):
    return jnp.dot(left_rows, block_rows, preferred_element_type=jnp.float32)


def column_maker(left_rows, block_rows):
    return lax.dot_general(
        left_rows, block_rows, (((1,), (1,)), ((), ())), preferred_element_type=jnp.float32
    )


def attend_block(
    carry_state, query_rows, query_pos, key_rows, value_rows, key_pos, key_ok, rel_rows
):
    row_top, row_total, weighted = carry_state
    head_count = rel_rows.shape[0]
    query_count = query_rows.shape[0]
    query_heads = query_rows.reshape(query_count, head_count, -1)
    key_heads = key_rows.reshape(key_rows.shape[0], head_count, -1)
    value_heads = value_rows.reshape(value_rows.shape[0], head_count, -1)
    span_size = (rel_rows.shape[1] + 1) // 2
    scores = jnp.einsum("qhd,khd->hqk", query_heads, key_heads, preferred_element_type=jnp.float32)
    offset = key_pos[None, :] - query_pos[:, None] + (span_size - 1)
    scores = scores + jnp.take(rel_rows, offset, axis=1)
    allowed = key_ok[None, None, :]
    new_top = jnp.maximum(row_top, jnp.max(jnp.where(allowed, scores, FLOOR_SCORE), axis=2))
    weights = jnp.where(allowed, jnp.exp(scores - new_top[:, :, None]), 0.0)
    rescale = jnp.exp(row_top - new_top)
    row_total = row_total * rescale + jnp.sum(weights, axis=2)
    update = jnp.einsum(
        "hqk,khd->qhd",
        weights.astype(jnp.bfloat16),
        value_heads,
        preferred_element_type=jnp.float32,
    )
    weighted = (
        weighted.reshape(query_count, head_count, -1) * jnp.transpose(rescale)[:, :, None] + update
    )
    return (new_top, row_total, weighted.reshape(query_count, -1))


def visit_block(
    carry_state, query_rows, query_pos, key_rows, value_rows, key_pos, key_ok, rel_rows
):
    return attend_block(
        carry_state, query_rows, query_pos, key_rows, value_rows, key_pos, key_ok, rel_rows
    )


def local_keys(
    carry_state,
    query_rows,
    query_pos,
    cache_rows,
    cache_vals,
    cache_pos,
    cache_ok,
    new_rows,
    new_vals,
    new_pos,
    new_ok,
    rel_rows,
):
    total_rows = cache_rows.shape[0]
    block_size = min(512, total_rows)
    block_count = total_rows // block_size

    def scan_step(carried, block_item):
        block_keys, block_values, block_pos, block_ok = block_item
        return (
            visit_block(
                carried,
                query_rows,
                query_pos,
                block_keys,
                block_values,
                block_pos,
                block_ok,
                rel_rows,
            ),
            None,
        )

    blocks = (
        cache_rows.reshape(block_count, block_size, -1),
        cache_vals.reshape(block_count, block_size, -1),
        cache_pos.reshape(block_count, block_size),
        cache_ok.reshape(block_count, block_size),
    )
    carry_state, unused = lax.scan(scan_step, carry_state, blocks)
    return visit_block(
        carry_state, query_rows, query_pos, new_rows, new_vals, new_pos, new_ok, rel_rows
    )


def shards(
    tokens,
    cache_keys,
    cache_values,
    joined_weight,
    output_weight,
    upward_weight,
    downward_weight,
    first_gain,
    second_gain,
    bias_table,
    bucket_index,
    cached_lengths,
    new_counts,
    extend_flags,
):
    tensor_size = lax.axis_size("tensor")
    seq_index = lax.axis_index("seq")
    tensor_index = lax.axis_index("tensor")
    new_rows = tokens.shape[0]
    cache_count = cache_keys.shape[0]
    used_len = cached_lengths[seq_index] * extend_flags[seq_index]
    new_count = new_counts[seq_index]
    attn_width = output_weight.shape[1]
    local_width = attn_width // tensor_size
    head_count = bias_table.shape[1]
    trainer_rows = joined_weight.shape[0]
    joined_send = joined_weight.reshape(trainer_rows, 3, tensor_size, local_width)
    joined_send = (
        jnp.transpose(joined_send, (0, 2, 1, 3))
        .reshape(trainer_rows, 3 * attn_width)
        .astype(jnp.bfloat16)
    )
    joined_mine, output_mine, upward_mine, downward_mine = (
        lax.all_to_all(joined_send, "tensor", split_axis=1, concat_axis=0, tiled=True),
        lax.all_to_all(
            output_weight.astype(jnp.bfloat16), "tensor", split_axis=1, concat_axis=0, tiled=True
        ),
        lax.all_to_all(
            upward_weight.astype(jnp.bfloat16), "tensor", split_axis=1, concat_axis=0, tiled=True
        ),
        lax.all_to_all(
            downward_weight.astype(jnp.bfloat16), "tensor", split_axis=1, concat_axis=0, tiled=True
        ),
    )
    normed = rms_rows(tokens, first_gain)
    projected = row_adder(normed, lax.all_gather(joined_mine, "seq", axis=0, tiled=True)).astype(
        jnp.bfloat16
    )
    query_rows = projected[:, :local_width]
    key_new = projected[:, local_width : 2 * local_width]
    value_new = projected[:, 2 * local_width :]
    bucket_hot = (
        bucket_index[:, None] == jnp.arange(bias_table.shape[0], dtype=jnp.int32)[None, :]
    ).astype(jnp.float32)
    rel_rows = jnp.einsum("bh,lb->hl", bias_table, bucket_hot, precision=lax.Precision.HIGHEST)
    cache_pos = jnp.arange(cache_count, dtype=jnp.int32)
    cache_ok = cache_pos < used_len
    new_slots = jnp.arange(new_rows, dtype=jnp.int32)
    new_pos = used_len + new_slots
    new_ok = new_slots < new_count
    empty_state = (
        jnp.full((head_count, new_rows), FLOOR_SCORE, jnp.float32),
        jnp.zeros((head_count, new_rows), jnp.float32),
        jnp.zeros((new_rows, local_width), jnp.float32),
    )
    final_top, final_total, final_sum = local_keys(
        empty_state,
        query_rows,
        new_pos,
        cache_keys,
        cache_values,
        cache_pos,
        cache_ok,
        key_new,
        value_new,
        new_pos,
        new_ok,
        rel_rows,
    )
    attention = final_sum.reshape(new_rows, head_count, -1) / jnp.transpose(final_total)[:, :, None]
    attention = attention.reshape(new_rows, local_width).astype(jnp.bfloat16)
    attended = column_maker(attention, lax.all_gather(output_mine, "seq", axis=0, tiled=True))
    share_rows = new_rows // tensor_size
    row_start = tensor_index * share_rows
    summed = lax.psum(attended.astype(jnp.bfloat16), "tensor").astype(jnp.float32)
    hidden = tokens.astype(jnp.float32) + summed
    normed_mid = rms_rows(hidden, second_gain)
    hidden_mine = lax.dynamic_slice_in_dim(hidden, row_start, share_rows, 0)
    inner = row_adder(normed_mid, lax.all_gather(upward_mine, "seq", axis=0, tiled=True))
    active = jax.nn.relu(inner).astype(jnp.bfloat16)
    feed_out = column_maker(active, lax.all_gather(downward_mine, "seq", axis=0, tiled=True))
    feed_mine = lax.psum_scatter(
        feed_out.astype(jnp.bfloat16), "tensor", scatter_dimension=0, tiled=True
    ).astype(jnp.float32)
    return (hidden_mine + feed_mine).astype(jnp.bfloat16)


def solution(mesh):
    return jax.shard_map(
        shards,
        mesh=mesh,
        in_specs=(
            P("seq", None),
            P("seq", "tensor"),
            P("seq", "tensor"),
            P(("seq", "tensor"), None),
            P(("seq", "tensor"), None),
            P(("seq", "tensor"), None),
            P(("seq", "tensor"), None),
            P(),
            P(),
            P(None, "tensor"),
            P(),
            P(),
            P(),
            P(),
        ),
        out_specs=P(("seq", "tensor"), None),
        check_vma=False,
    )
```

profile of v0, /device:TPU:0, one launch (start us, length us, event | category | flops | bytes accessed | tf_op | source)
XLA Modules:
  0.0 660.5 jit_solution(6525563530860254248)
XLA Ops:
  6.5 1.1 convert_element_type.69
  7.6 0.0 copy-start.14
  7.6 0.1 convert_element_type.70
  7.8 0.1 copy.96
  7.9 0.9 convert_element_type.72
  8.8 6.3 all-to-all-start
  15.1 0.6 dynamic_slice.23
  15.7 0.6 dynamic_slice.24
  17.6 0.2 fusion.29
  17.8 0.1 copy.88
  18.0 0.6 copy.97
  18.6 4.0 all-to-all-done
  22.6 3.3 all-to-all-start.1
  25.9 0.0 all-gather.4.cloned.1.call-start
  26.0 0.7 all-gather.4.cloned.1.call-update
  26.6 0.0 all-reduce.2.cloned.1.call-start
  26.7 0.4 convolution_bitcast_fusion.2
  27.1 0.2 copy.64
  27.4 217.1 %gather_fusion = f32[65536,4]{1,0:T(8,128)} fusion(f32[4,1023]{0,1:T(8,128)S(1)} %copy.64, s32[65536]{0:T(1024)S(1)} %broadcast_clamp_fusion.1), kind=kCustom, calls=%fused_computation.clone | custom fusion | bytes 2359296 | tf_op jit(solution)/shard_map/while/body/eval_jaxpr/jit(_take)/gather | solution.py:38
  244.5 19.0 %copy.66 = f32[256,256,4]{0,1,2:T(8,128)S(1)} copy(f32[256,256,4]{2,1,0:T(8,128)} %bitcast.99) | data formatting | bytes 2097152 | tf_op jit(solution)/shard_map/while/body/eval_jaxpr/jit(_take)/gather | solution.py:38
  263.5 0.3 fusion.36
  263.8 0.8 copy.63
  264.5 0.8 copy.62
  265.3 0.1 copy.89
  265.5 217.1 %gather_fusion.1 = f32[65536,4]{1,0:T(8,128)} fusion(f32[4,1023]{0,1:T(8,128)S(1)} %copy.64, s32[65536]{0:T(1024)S(1)} %broadcast_clamp_fusion), kind=kCustom, calls=%fused_computation.1.clone | custom fusion | bytes 2359296 | tf_op jit(solution)/shard_map/jit(_take)/gather | solution.py:38
  482.6 19.1 %copy.73 = f32[256,256,4]{0,1,2:T(8,128)S(1)} copy(f32[256,256,4]{2,1,0:T(8,128)} %bitcast.98) | data formatting | bytes 2097152 | tf_op jit(solution)/shard_map/jit(_take)/gather | solution.py:38
  501.7 0.8 copy.70
  502.5 0.6 dynamic_slice.25
  503.1 0.8 copy.67
  503.8 0.2 fusion.6
  504.0 0.6 iota_compare_fusion.2
  504.7 9.9 %all_gather.13 = bf16[1024,256]{1,0:T(8,128)(2,1)S(1)} all-gather(bf16[128,256]{1,0:T(8,128)(2,1)S(1)} %bitcast.115), channel_id=1, replica_groups=mesh['seq'=8,'tensor'=4] {'seq'}, dimensions={0}, use_global_device_ids=true | all-gather | bytes 589824 | tf_op jit(solution)/shard_map/all_gather | solution.py:192
  514.5 2.0 convolution_convert_fusion.2
  516.6 0.7 fusion.47
  517.2 1.0 copy.61
  518.3 0.8 copy.69
  519.0 0.7 copy.74
  519.8 1.4 select_reduce_fusion.1
  521.2 0.0 copy-start.7
  521.2 0.4 select_reduce_fusion
  521.6 0.4 fusion.9
  522.1 0.3 fusion.4
  522.4 0.0 copy-start.4
  522.4 0.1 copy-done.13
  522.5 0.3 fusion.5
  522.8 0.0 copy-start.5
  522.9 1.2 convolution_convert_fusion
  524.0 0.0 all-reduce.2.cloned.1.call-update
  524.0 0.0 all-gather.6.cloned.1.call-start
  524.2 20.1 %all_to_all.73 = bf16[32,4,1024]{2,0,1:T(8,128)(2,1)} all-to-all(bf16[32,4,1024]{2,0,1:T(8,128)(2,1)S(1)} %bitcast.109), channel_id=1, replica_groups=mesh['seq'=8,'tensor'=4] {'tensor'}, dimensions={1} | all-to-all | bytes 524288 | tf_op jit(solution)/shard_map/all_to_all | solution.py:148
  544.3 0.0 all-gather.6.cloned.1.call-update
  544.3 0.0 copy-start.16
  544.3 0.0 all-gather.8.cloned.1.call-start
  544.4 11.8 %all_to_all.74 = bf16[32,4,1024]{2,0,1:T(8,128)(2,1)} all-to-all(bf16[32,4,1024]{2,0,1:T(8,128)(2,1)S(1)} %bitcast.110), channel_id=1, replica_groups=mesh['seq'=8,'tensor'=4] {'tensor'}, dimensions={1} | all-to-all | bytes 524288 | tf_op jit(solution)/shard_map/all_to_all | solution.py:151
  556.2 0.0 all-gather.8.cloned.1.call-update
  556.2 0.0 reduce-scatter.2.cloned.1.call-start
  556.2 10.4 %all-reduce.2.cloned.1.call-done = bf16[256,1024]{1,0:T(8,128)(2,1)} async-done(((bf16[256,1024]{1,0:T(8,128)(2,1)}), bf16[256,1024]{1,0:T(8,128)(2,1)}) %all-reduce.2.cloned.1.call-update) | async-done | bytes 524304 | tf_op jit(solution)/shard_map/psum | solution.py:195
  566.6 1.4 convert_add_fusion
  568.0 28.4 %all-gather.6.cloned.1.call-done = bf16[1024,1024]{1,0:T(8,128)(2,1)} async-done(((bf16[128,1024]{1,0:T(8,128)(2,1)}), bf16[1024,1024]{1,0:T(8,128)(2,1)}) %all-gather.6.cloned.1.call-update) | async-done | bytes 2097168 | tf_op jit(solution)/shard_map/all_gather | solution.py:199
  596.5 29.7 %all-gather.8.cloned.1.call-done = bf16[1024,1024]{1,0:T(8,128)(2,1)} async-done(((bf16[128,1024]{1,0:T(8,128)(2,1)}), bf16[1024,1024]{1,0:T(8,128)(2,1)}) %all-gather.8.cloned.1.call-update) | async-done | bytes 2097168 | tf_op jit(solution)/shard_map/all_gather | solution.py:201
  626.1 4.4 convolution_convert_fusion.1
  630.5 0.0 reduce-scatter.2.cloned.1.call-update
  630.6 21.8 %reduce-scatter.2.cloned.1.call-done = bf16[64,1024]{1,0:T(8,128)(2,1)} async-done(((bf16[256,1024]{1,0:T(8,128)(2,1)}), bf16[64,1024]{1,0:T(8,128)(2,1)}) %reduce-scatter.2.cloned.1.call-update) | async-done | bytes 131088 | tf_op jit(solution)/shard_map/reduce_scatter | solution.py:202
  652.4 1.6 add_convert_fusion
  (49 shorter events, 0.3 us)
Async XLA Ops:
  6.5 20.1 %copy-start = (f32[32,4]{0,1:T(4,128)S(1)}, f32[32,4]{0,1:T(4,128)}, u32[]{:S(2)}) copy-start(f32[32,4]{0,1:T(4,128)} %param.25) | copy-start | bytes 1540
  6.5 8.6 %copy-start.17 = (s32[8]{0:T(128)S(1)}, s32[8]{0:T(128)}, u32[]{:S(2)}) copy-start(s32[8]{0:T(128)} %param.27) | copy-start | bytes 100
  6.5 9.1 %copy-start.18 = (s32[8]{0:T(128)S(1)}, s32[8]{0:T(128)}, u32[]{:S(2)}) copy-start(s32[8]{0:T(128)} %param.29) | copy-start | bytes 100
  6.5 11.4 %copy-start.10 = (f32[32,1024]{1,0:T(8,128)S(1)}, f32[32,1024]{1,0:T(8,128)}, u32[]{:S(2)}) copy-start(f32[32,1024]{1,0:T(8,128)} %param.20) | copy-start | bytes 393220
  7.6 19.1 %copy-start.14 = (s32[1023]{0:T(1024)S(1)}, s32[1023]{0:T(1024)}, u32[]{:S(2)}) copy-start(s32[1023]{0:T(1024)} %param.26) | copy-start | bytes 12280
  8.8 13.8 %all-to-all-start = ((bf16[32,4,768]{2,0,1:T(8,128)(2,1)}), bf16[32,4,768]{2,0,1:T(8,128)(2,1)S(1)}, u32[]{:S(2)}, u32[]{:S(2)}) async-start(bf16[32,4,768]{2,0,1:T(8,128)(2,1)} %convert_element_type.72), calls=%async_computation | async-start | bytes 393216 | tf_op jit(solution)/shard_map/all_to_all | solution.py:144
  22.6 3.3 copy-start.3
  22.6 482.1 %all-to-all-start.1 = ((bf16[32,4,256]{2,0,1:T(8,128)(2,1)}), bf16[32,4,256]{2,0,1:T(8,128)(2,1)S(1)}, u32[]{:S(2)}, u32[]{:S(2)}) async-start(bf16[32,4,256]{2,0,1:T(8,128)(2,1)} %bitcast.97), calls=%async_computation.1 | async-start | bytes 131072 | tf_op jit(solution)/shard_map/all_to_all | solution.py:145
  25.9 488.6 %all-gather.4.cloned.1.call-start = ((), (), s32[]{:S(2)}) async-start(), calls=%async_computation.5 | async-start | bytes 1769472 | tf_op jit(solution)/shard_map/all_gather | solution.py:156
  26.6 540.0 %all-reduce.2.cloned.1.call-start = ((), (), s32[]{:S(2)}) async-start(), calls=%async_computation.6 | async-start | bytes 1048576 | tf_op jit(solution)/shard_map/psum | solution.py:195
  244.5 20.1 %copy-start.11 = (bf16[256,256]{1,0:T(8,128)(2,1)S(1)}, bf16[256,256]{1,0:T(8,128)(2,1)}, u32[]{:S(2)}) copy-start(bf16[256,256]{1,0:T(8,128)(2,1)} %param.17) | copy-start | bytes 393220
  482.6 19.9 %copy-start.19 = (s32[8]{0:T(128)S(1)}, s32[8]{0:T(128)}, u32[]{:S(2)}) copy-start(s32[8]{0:T(128)} %param.28) | copy-start | bytes 100
  482.6 20.5 %copy-start.12 = (bf16[256,256]{1,0:T(8,128)(2,1)S(1)}, bf16[256,256]{1,0:T(8,128)(2,1)}, u32[]{:S(2)}) copy-start(bf16[256,256]{1,0:T(8,128)(2,1)} %param.18) | copy-start | bytes 393220
  482.6 21.2 %copy-start.2 = (bf16[256,1024]{1,0:T(8,128)(2,1)S(1)}, bf16[256,1024]{1,0:T(8,128)(2,1)}, u32[]{:S(2)}) copy-start(bf16[256,1024]{1,0:T(8,128)(2,1)} %param.16) | copy-start | bytes 1572868
  482.6 31.9 %copy-start.15 = (f32[1024]{0:T(1024)S(1)}, f32[1024]{0:T(1024)}, u32[]{:S(2)}) copy-start(f32[1024]{0:T(1024)} %param.23) | copy-start | bytes 12292
  519.0 2.1 copy-start.8
  519.8 1.4 copy-start.9
  521.2 0.9 copy-start.7
  521.6 0.9 copy-start.13
  522.4 1.7 copy-start.4
  522.8 21.5 %copy-start.5 = (f32[32,4096]{1,0:T(8,128)S(1)}, f32[32,4096]{1,0:T(8,128)}, u32[]{:S(2)}) copy-start(f32[32,4096]{1,0:T(8,128)} %param.22) | copy-start | bytes 1572868
  524.0 72.4 %all-gather.6.cloned.1.call-start = ((), (), s32[]{:S(2)}) async-start(), calls=%async_computation.7 | async-start | bytes 2359296 | tf_op jit(solution)/shard_map/all_gather | solution.py:199
  544.3 81.8 %copy-start.16 = (f32[1024]{0:T(1024)S(1)}, f32[1024]{0:T(1024)}, u32[]{:S(2)}) copy-start(f32[1024]{0:T(1024)} %param.24) | copy-start | bytes 12292
  544.3 81.8 %all-gather.8.cloned.1.call-start = ((), (), s32[]{:S(2)}) async-start(), calls=%async_computation.8 | async-start | bytes 2359296 | tf_op jit(solution)/shard_map/all_gather | solution.py:201
  556.2 96.2 %reduce-scatter.2.cloned.1.call-start = ((), (), s32[]{:S(2)}) async-start(), calls=%async_computation.9 | async-start | bytes 655360 | tf_op jit(solution)/shard_map/reduce_scatter | solution.py:202
  566.6 59.5 %copy-start.6 = (bf16[256,1024]{1,0:T(8,128)(2,1)S(1)}, bf16[256,1024]{1,0:T(8,128)(2,1)}, u32[]{:S(2)}) copy-start(bf16[256,1024]{1,0:T(8,128)(2,1)} %all-reduce.2.cloned.1.call-done) | copy-start | bytes 1572868
  626.1 27.8 %copy-start.1 = (f32[32,4]{0,1:T(4,128)S(1)}, f32[32,4]{0,1:T(4,128)}, u32[]{:S(2)}) copy-start(f32[32,4]{0,1:T(4,128)} %param.25) | copy-start | bytes 1540
Sparse Core Ops, SparseCore 0:
  28.6 27.1 all-gather.3
  524.2 42.4 all-reduce.1
  568.5 27.8 all-gather.5
  598.2 27.8 all-gather.7
  630.7 21.6 reduce-scatter.1
where the time goes:
time: 661 us; the launch traced here: 660 us
  local copies, waits for them, and re-layouts  483 us (73%)
  waiting for transfers between devices  95 us (14%)
  blocking collectives  41.7 us (6%)
  between operations  14.8 us (2%)
  matrix products  10.4 us (2%)
  starting transfers between devices  9.81 us (1%)
    gather x4, local copies, waits for them, and re-layouts, attend_block(): scores = scores + jnp.take(rel_rows, offset, axis=1)  472 us
    all_gather x1, waiting for transfers between devices, shards(): lax.all_gather(downward_mine, 'seq', axis=0, tiled=True)  29.7 us
    all_gather x1, waiting for transfers between devices, shards(): lax.all_gather(upward_mine, 'seq', axis=0, tiled=True)  28.4 us
    reduce_scatter x1, waiting for transfers between devices, shards(): lax.psum_scatter(feed_out.astype(jnp.bfloat16), 'tensor', scatter_dimensi...  21.8 us
    all_to_all x1, blocking collectives, shards(): lax.all_to_all(upward_weight.astype(jnp.bfloat16), 'tensor', split_axis=1...  20.1 us
  transfers between devices with their start and end apart: 7, of which 5 were waited for; matrix products, arithmetic and copies ran while one was open for 73% of the time, Pallas kernels for 0%

commit v1 on v0

--- a/solution.py
+++ b/solution.py
@@ -5,6 +5,18 @@
 
 EPSILON = 1e-06
 FLOOR_SCORE = -1e30
+
+
+def doubled_up(array, axis, dim):
+    ways, here = (lax.axis_size(axis), lax.axis_index(axis))
+    grown, reach = (array, 1)
+    while reach < ways:
+        theirs = lax.ppermute(grown, axis, [(d, d ^ reach) for d in range(ways)])
+        mine_first = jnp.concatenate([grown, theirs], axis=dim)
+        theirs_first = jnp.concatenate([theirs, grown], axis=dim)
+        grown = jnp.where(here & reach == 0, mine_first, theirs_first)
+        reach = 2 * reach
+    return grown
 
 
 def rms_rows(rows, gain):
@@ -198,7 +210,7 @@
     hidden_mine = lax.dynamic_slice_in_dim(hidden, row_start, share_rows, 0)
     inner = row_adder(normed_mid, lax.all_gather(upward_mine, "seq", axis=0, tiled=True))
     active = jax.nn.relu(inner).astype(jnp.bfloat16)
-    feed_out = column_maker(active, lax.all_gather(downward_mine, "seq", axis=0, tiled=True))
+    feed_out = column_maker(active, doubled_up(downward_mine, "seq", 0))
     feed_mine = lax.psum_scatter(
         feed_out.astype(jnp.bfloat16), "tensor", scatter_dimension=0, tiled=True
     ).astype(jnp.float32)

time: 661 us -> 639 us (0.967)
  waiting for transfers between devices: 95 us -> 70.3 us
    ppermute x0 -> x3, waiting for transfers between devices: none -> 44.6 us  [doubled_up(): theirs = lax.ppermute(grown, axis, [(d, d ^ reach) for d in range(ways)])]
    all_gather x1 -> x0, waiting for transfers between devices: 29.7 us -> none  [shards(): lax.all_gather(downward_mine, 'seq', axis=0, tiled=True)]
    all_gather x1, waiting for transfers between devices: 28.4 us -> 0.05 us  [shards(): lax.all_gather(upward_mine, 'seq', axis=0, tiled=True)]
    psum x1, waiting for transfers between devices: 10.4 us -> 0.01 us  [shards(): lax.psum(attended.astype(jnp.bfloat16), 'tensor').astype(jnp.float32)]
  transfers between devices with their start and end apart: 7 -> 9, of which waited for: 5 -> 6; matrix products, arithmetic and copies ran while one was open for 73% -> 76% of each run, Pallas kernels for 0% -> 0%
where the time goes in v1:
time: 639 us; the launch traced here: 638 us
  local copies, waits for them, and re-layouts  483 us (76%)
  waiting for transfers between devices  70.3 us (11%)
  blocking collectives  41.2 us (6%)
  between operations  14.8 us (2%)
  starting transfers between devices  12.3 us (2%)
  matrix products  10.4 us (2%)
  other arithmetic  6.46 us (1%)
    gather x4, local copies, waits for them, and re-layouts, attend_block(): scores = scores + jnp.take(rel_rows, offset, axis=1)  472 us
    ppermute x3, waiting for transfers between devices, doubled_up(): theirs = lax.ppermute(grown, axis, [(d, d ^ reach) for d in range(ways)])  44.6 us
    reduce_scatter x1, waiting for transfers between devices, shards(): lax.psum_scatter(feed_out.astype(jnp.bfloat16), 'tensor', scatter_dimensi...  20.9 us
    all_to_all x1, blocking collectives, shards(): lax.all_to_all(upward_weight.astype(jnp.bfloat16), 'tensor', split_axis=1...  20.1 us
  transfers between devices with their start and end apart: 9, of which 6 were waited for; matrix products, arithmetic and copies ran while one was open for 76% of the time, Pallas kernels for 0%

profile of v1, /device:TPU:0, one launch (start us, length us, event | category | flops | bytes accessed | tf_op | source)
XLA Modules:
  0.0 638.2 jit_solution(548631739487405836)
XLA Ops:
  6.5 1.1 convert_element_type.69
  7.6 0.0 copy-start.14
  7.6 0.1 convert_element_type.70
  7.8 0.1 copy.96
  7.9 0.9 convert_element_type.72
  8.8 6.3 all-to-all-start
  15.1 0.6 dynamic_slice.23
  15.7 0.6 dynamic_slice.24
  17.6 0.2 fusion.37
  17.8 0.1 copy.88
  18.0 0.6 copy.97
  18.6 4.0 all-to-all-done
  22.6 3.3 all-to-all-start.1
  25.9 0.0 all-gather.3.cloned.1.call-start
  26.0 0.7 all-gather.3.cloned.1.call-update
  26.6 0.0 all-reduce.2.cloned.1.call-start
  26.7 0.4 convolution_bitcast_fusion.2
  27.1 0.2 copy.64
  27.4 217.1 %gather_fusion = f32[65536,4]{1,0:T(8,128)} fusion(f32[4,1023]{0,1:T(8,128)S(1)} %copy.64, s32[65536]{0:T(1024)S(1)} %broadcast_clamp_fusion.1), kind=kCustom, calls=%fused_computation.clone | custom fusion | bytes 2359296 | tf_op jit(solution)/shard_map/while/body/eval_jaxpr/jit(_take)/gather | solution.py:50
  244.5 19.0 %copy.66 = f32[256,256,4]{0,1,2:T(8,128)S(1)} copy(f32[256,256,4]{2,1,0:T(8,128)} %bitcast.98) | data formatting | bytes 2097152 | tf_op jit(solution)/shard_map/while/body/eval_jaxpr/jit(_take)/gather | solution.py:50
  263.5 0.3 fusion.44
  263.8 0.8 copy.63
  264.5 0.8 copy.62
  265.3 0.1 copy.89
  265.5 217.1 %gather_fusion.1 = f32[65536,4]{1,0:T(8,128)} fusion(f32[4,1023]{0,1:T(8,128)S(1)} %copy.64, s32[65536]{0:T(1024)S(1)} %broadcast_clamp_fusion), kind=kCustom, calls=%fused_computation.1.clone | custom fusion | bytes 2359296 | tf_op jit(solution)/shard_map/jit(_take)/gather | solution.py:50
  482.6 19.1 %copy.73 = f32[256,256,4]{0,1,2:T(8,128)S(1)} copy(f32[256,256,4]{2,1,0:T(8,128)} %bitcast.97) | data formatting | bytes 2097152 | tf_op jit(solution)/shard_map/jit(_take)/gather | solution.py:50
  501.7 0.8 copy.70
  502.5 0.6 dynamic_slice.25
  503.1 0.8 copy.67
  503.8 0.2 fusion.14
  504.0 0.6 iota_compare_fusion.2
  504.7 9.9 %all_gather.10 = bf16[1024,256]{1,0:T(8,128)(2,1)S(1)} all-gather(bf16[128,256]{1,0:T(8,128)(2,1)S(1)} %bitcast.115), channel_id=1, replica_groups=mesh['seq'=8,'tensor'=4] {'seq'}, dimensions={0}, use_global_device_ids=true | all-gather | bytes 589824 | tf_op jit(solution)/shard_map/all_gather | solution.py:204
  514.5 2.0 convolution_convert_fusion.1
  516.6 0.7 fusion.56
  517.2 1.0 copy.61
  518.3 0.8 copy.69
  519.0 0.7 copy.74
  519.8 1.4 select_reduce_fusion.1
  521.2 0.0 copy-start.7
  521.2 0.4 select_reduce_fusion
  521.6 0.4 fusion.17
  522.1 0.3 fusion.12
  522.4 0.1 copy-done.13
  522.5 0.3 fusion.13
  522.9 1.1 convolution_convert_fusion
  524.0 0.0 all-reduce.2.cloned.1.call-update
  524.0 0.0 all-gather.5.cloned.1.call-start
  524.1 20.1 %all_to_all.73 = bf16[32,4,1024]{2,0,1:T(8,128)(2,1)} all-to-all(bf16[32,4,1024]{2,0,1:T(8,128)(2,1)S(1)} %bitcast.107), channel_id=1, replica_groups=mesh['seq'=8,'tensor'=4] {'tensor'}, dimensions={1} | all-to-all | bytes 524288 | tf_op jit(solution)/shard_map/all_to_all | solution.py:160
  544.2 0.0 all-gather.5.cloned.1.call-update
  544.3 0.0 reduce-scatter.2.cloned.1.call-start
  544.4 11.3 %all_to_all.74 = bf16[32,4,1024]{2,0,1:T(8,128)(2,1)S(1)} all-to-all(bf16[32,4,1024]{2,0,1:T(8,128)(2,1)S(1)} %bitcast.108), channel_id=1, replica_groups=mesh['seq'=8,'tensor'=4] {'tensor'}, dimensions={1} | all-to-all | bytes 524288 | tf_op jit(solution)/shard_map/all_to_all | solution.py:163
  555.6 1.5 collective-permute-done
  557.2 0.1 maximum_select_fusion.5
  557.3 1.4 collective-permute-start.1
  558.7 12.7 %collective-permute-done.1 = bf16[256,1024]{1,0:T(8,128)(2,1)S(1)} collective-permute-done((bf16[256,1024]{1,0:T(8,128)(2,1)S(1)}, bf16[256,1024]{1,0:T(8,128)(2,1)S(1)}, u32[]{:S(2)}, u32[]{:S(2)}) %collective-permute-start.1) | collective-permute-done | bytes 524320 | tf_op jit(solution)/shard_map/ppermute | solution.py:14
  571.3 0.5 maximum_select_fusion.4
  571.8 1.2 collective-permute-start.2
  573.0 1.4 convert_add_fusion
  574.4 30.4 %collective-permute-done.2 = bf16[512,1024]{1,0:T(8,128)(2,1)} collective-permute-done((bf16[512,1024]{1,0:T(8,128)(2,1)S(1)}, bf16[512,1024]{1,0:T(8,128)(2,1)}, u32[]{:S(2)}, u32[]{:S(2)}) %collective-permute-start.2) | collective-permute-done | bytes 1048608 | tf_op jit(solution)/shard_map/ppermute | solution.py:14
  604.8 0.1 all-gather.5.cloned.1.call-done
  604.9 4.3 fusion.7
  609.2 0.0 reduce-scatter.2.cloned.1.call-update
  609.2 20.9 %reduce-scatter.2.cloned.1.call-done = bf16[64,1024]{1,0:T(8,128)(2,1)} async-done(((bf16[256,1024]{1,0:T(8,128)(2,1)}), bf16[64,1024]{1,0:T(8,128)(2,1)}) %reduce-scatter.2.cloned.1.call-update) | async-done | bytes 131088 | tf_op jit(solution)/shard_map/reduce_scatter | solution.py:214
  630.1 1.6 add_convert_fusion
  (54 shorter events, 0.3 us)
Async XLA Ops:
  6.5 20.1 %copy-start = (f32[32,4]{0,1:T(4,128)S(1)}, f32[32,4]{0,1:T(4,128)}, u32[]{:S(2)}) copy-start(f32[32,4]{0,1:T(4,128)} %param.25) | copy-start | bytes 1540
  6.5 8.6 %copy-start.17 = (s32[8]{0:T(128)S(1)}, s32[8]{0:T(128)}, u32[]{:S(2)}) copy-start(s32[8]{0:T(128)} %param.27) | copy-start | bytes 100
  6.5 9.1 %copy-start.18 = (s32[8]{0:T(128)S(1)}, s32[8]{0:T(128)}, u32[]{:S(2)}) copy-start(s32[8]{0:T(128)} %param.29) | copy-start | bytes 100
  6.5 11.4 %copy-start.10 = (f32[32,1024]{1,0:T(8,128)S(1)}, f32[32,1024]{1,0:T(8,128)}, u32[]{:S(2)}) copy-start(f32[32,1024]{1,0:T(8,128)} %param.20) | copy-start | bytes 393220
  7.6 19.1 %copy-start.14 = (s32[1023]{0:T(1024)S(1)}, s32[1023]{0:T(1024)}, u32[]{:S(2)}) copy-start(s32[1023]{0:T(1024)} %param.26) | copy-start | bytes 12280
  8.8 13.8 %all-to-all-start = ((bf16[32,4,768]{2,0,1:T(8,128)(2,1)}), bf16[32,4,768]{2,0,1:T(8,128)(2,1)S(1)}, u32[]{:S(2)}, u32[]{:S(2)}) async-start(bf16[32,4,768]{2,0,1:T(8,128)(2,1)} %convert_element_type.72), calls=%async_computation | async-start | bytes 393216 | tf_op jit(solution)/shard_map/all_to_all | solution.py:156
  22.6 3.3 copy-start.3
  22.6 482.1 %all-to-all-start.1 = ((bf16[32,4,256]{2,0,1:T(8,128)(2,1)}), bf16[32,4,256]{2,0,1:T(8,128)(2,1)S(1)}, u32[]{:S(2)}, u32[]{:S(2)}) async-start(bf16[32,4,256]{2,0,1:T(8,128)(2,1)} %bitcast.96), calls=%async_computation.1 | async-start | bytes 131072 | tf_op jit(solution)/shard_map/all_to_all | solution.py:157
  25.9 488.6 %all-gather.3.cloned.1.call-start = ((), (), s32[]{:S(2)}) async-start(), calls=%async_computation.5 | async-start | bytes 1769472 | tf_op jit(solution)/shard_map/all_gather | solution.py:168
  26.6 546.4 %all-reduce.2.cloned.1.call-start = ((), (), s32[]{:S(2)}) async-start(), calls=%async_computation.6 | async-start | bytes 1048576 | tf_op jit(solution)/shard_map/psum | solution.py:207
  244.5 20.1 %copy-start.11 = (bf16[256,256]{1,0:T(8,128)(2,1)S(1)}, bf16[256,256]{1,0:T(8,128)(2,1)}, u32[]{:S(2)}) copy-start(bf16[256,256]{1,0:T(8,128)(2,1)} %param.17) | copy-start | bytes 393220
  482.6 19.9 %copy-start.19 = (s32[8]{0:T(128)S(1)}, s32[8]{0:T(128)}, u32[]{:S(2)}) copy-start(s32[8]{0:T(128)} %param.28) | copy-start | bytes 100
  482.6 20.5 %copy-start.12 = (bf16[256,256]{1,0:T(8,128)(2,1)S(1)}, bf16[256,256]{1,0:T(8,128)(2,1)}, u32[]{:S(2)}) copy-start(bf16[256,256]{1,0:T(8,128)(2,1)} %param.18) | copy-start | bytes 393220
  482.6 21.2 %copy-start.2 = (bf16[256,1024]{1,0:T(8,128)(2,1)S(1)}, bf16[256,1024]{1,0:T(8,128)(2,1)}, u32[]{:S(2)}) copy-start(bf16[256,1024]{1,0:T(8,128)(2,1)} %param.16) | copy-start | bytes 1572868
  482.6 31.9 %copy-start.15 = (f32[1024]{0:T(1024)S(1)}, f32[1024]{0:T(1024)}, u32[]{:S(2)}) copy-start(f32[1024]{0:T(1024)} %param.23) | copy-start | bytes 12292
  519.0 2.1 copy-start.8
  519.8 1.4 copy-start.9
  521.2 0.9 copy-start.7
  521.6 0.9 copy-start.13
  522.4 1.7 copy-start.4
  522.8 21.5 %copy-start.5 = (f32[32,4096]{1,0:T(8,128)S(1)}, f32[32,4096]{1,0:T(8,128)}, u32[]{:S(2)}) copy-start(f32[32,4096]{1,0:T(8,128)} %param.22) | copy-start | bytes 1572868
  524.0 80.8 %all-gather.5.cloned.1.call-start = ((), (), s32[]{:S(2)}) async-start(), calls=%async_computation.7 | async-start | bytes 2359296 | tf_op jit(solution)/shard_map/all_gather | solution.py:211
  544.3 85.8 %reduce-scatter.2.cloned.1.call-start = ((), (), s32[]{:S(2)}) async-start(), calls=%async_computation.8 | async-start | bytes 655360 | tf_op jit(solution)/shard_map/reduce_scatter | solution.py:214
  555.6 1.5 collective-permute-start
  557.3 14.0 %collective-permute-start.1 = (bf16[256,1024]{1,0:T(8,128)(2,1)S(1)}, bf16[256,1024]{1,0:T(8,128)(2,1)S(1)}, u32[]{:S(2)}, u32[]{:S(2)}) collective-permute-start(bf16[256,1024]{1,0:T(8,128)(2,1)S(1)} %maximum_select_fusion.5), channel_id=1, source_target_pairs={{0,8},{4,12},{8,0},{12,4},{16,24},{20,28},{24,16},{28,20},{1,9},{5... | collective-permute-start | bytes 1572872 | tf_op jit(solution)/shard_map/ppermute | solution.py:14
  558.7 46.2 %copy-start.16 = (f32[1024]{0:T(1024)S(1)}, f32[1024]{0:T(1024)}, u32[]{:S(2)}) copy-start(f32[1024]{0:T(1024)} %param.24) | copy-start | bytes 12292
  571.8 33.0 %collective-permute-start.2 = (bf16[512,1024]{1,0:T(8,128)(2,1)S(1)}, bf16[512,1024]{1,0:T(8,128)(2,1)}, u32[]{:S(2)}, u32[]{:S(2)}) collective-permute-start(bf16[512,1024]{1,0:T(8,128)(2,1)S(1)} %maximum_select_fusion.4), channel_id=1, source_target_pairs={{0,16},{4,20},{8,24},{12,28},{16,0},{20,4},{24,8},{28,12},{1,17},{... | collective-permute-start | bytes 3145736 | tf_op jit(solution)/shard_map/ppermute | solution.py:14
  573.0 31.9 %copy-start.6 = (bf16[256,1024]{1,0:T(8,128)(2,1)S(1)}, bf16[256,1024]{1,0:T(8,128)(2,1)}, u32[]{:S(2)}) copy-start(bf16[256,1024]{1,0:T(8,128)(2,1)} %all-reduce.2.cloned.1.call-done) | copy-start | bytes 1572868
  604.8 26.8 %copy-start.1 = (f32[32,4]{0,1:T(4,128)S(1)}, f32[32,4]{0,1:T(4,128)}, u32[]{:S(2)}) copy-start(f32[32,4]{0,1:T(4,128)} %param.25) | copy-start | bytes 1540
Sparse Core Ops, SparseCore 0:
  28.6 27.1 all-gather.2
  524.1 42.4 all-reduce.1
  568.5 36.2 all-gather.4
  609.3 20.7 reduce-scatter.1
